TPU v7x, 32 devices: a whole 2x2x4 slice. The times are simulated.
32 devices in a mesh: seq: 16 (over z, y, x), chan: 2 (over core).
Axes of the slice: x: 2, y: 2, z: 4, core: 2. Of those that a mesh axis runs over, the one named last changes fastest.
Arguments:
- streams: bfloat16 [3, 512, 4096], P(None, 'chan', 'seq'), may hold values from -6 to 6
- short_filters: float32 [3, 7, 512], P(None, None, 'chan'), may hold values from -2 to 2
- long_filter: float32 [64, 4096], P(None, 'seq'), may hold values from -2 to 2
- skip_gain: float32 [512], P('chan'), may hold values from 0.3 to 1.5
- out_grad: bfloat16 [512, 4096], P('chan', 'seq'), may hold values from -6 to 6
Outputs:
- stream_grad: bfloat16 [3, 512, 4096], P(None, 'chan', 'seq')
- filter_grad: float32 [64, 4096], P(None, 'seq')
All inputs are finite; a program needn't handle non-finite values.
Results may differ from a plain program's by a relative error of at most 0.0004.
Values may be sent and summed in bfloat16 or wider, within the bound.
A program may use at most 64 MiB of HBM per device.

v0:
```python
import math

import jax
import jax.numpy as jnp
from jax import lax
from jax.sharding import PartitionSpec as P


def partner_2(value, axis, apart):
    mask = 2**apart
    pairs = [(source, source ^ mask) for source in range(lax.axis_size(axis))]
    return lax.ppermute(value, axis, pairs)


def shifted(shard, axis, by):
    length = lax.axis_size(axis)
    pairs = [(i, i + by) for i in range(length) if 0 <= i + by < length]
    return lax.ppermute(shard, axis, pairs)


def rotate(real_part, imag_part, cosine, sine_part):
    return (real_part * cosine - imag_part * sine_part, real_part * sine_part + imag_part * cosine)


def split_halves(signal):
    middle = signal.shape[-1] // 2
    return (signal[..., :middle], signal[..., middle:])


def join_halves(real_part, imag_part):
    return jnp.concatenate([real_part, imag_part], axis=-1)


def complex_product(first_op, second_op, conjugate):
    first_re, first_im = split_halves(first_op)
    second_re, second_im = split_halves(second_op)
    if conjugate:
        second_im = -second_im
    return join_halves(
        first_re * second_re - first_im * second_im, first_re * second_im + first_im * second_re
    )


def dft_table(length, direction, scaling):
    indices = jnp.arange(length, dtype=jnp.int32)
    phases = (indices[:, None] * indices[None, :] % length).astype(jnp.float32) * (
        direction * 2.0 * math.pi / length
    )
    cosine = jnp.cos(phases) * scaling
    sine_part = jnp.sin(phases) * scaling
    upper_rows = jnp.concatenate([cosine, sine_part], axis=1)
    lower_rows = jnp.concatenate([-sine_part, cosine], axis=1)
    return jnp.concatenate([upper_rows, lower_rows], axis=0)


def section_count():
    return lax.axis_size("seq").bit_length() - 1


def bit_reverse(position, sections):
    result = jnp.zeros((), jnp.int32)
    for bit_level in range(sections):
        result = result + position // (1 << bit_level) % 2 * (1 << sections - 1 - bit_level)
    return result


def held_index():
    return bit_reverse(lax.axis_index("seq"), section_count())


def inner_twiddle(signal, held, direction):
    length = signal.shape[-1] // 2
    seq_total = length * lax.axis_size("seq")
    indices = jnp.arange(length, dtype=jnp.int32)
    phases = (indices * held % seq_total).astype(jnp.float32) * (
        direction * 2.0 * math.pi / seq_total
    )
    real_part, imag_part = split_halves(signal)
    turned_re, turned_im = rotate(real_part, imag_part, jnp.cos(phases), jnp.sin(phases))
    return join_halves(turned_re, turned_im)


def forward_sections(signal):
    position = lax.axis_index("seq")
    sections = section_count()
    for bit_level in reversed(range(sections)):
        half_span = 1 << bit_level
        partner = partner_2(signal, "seq", bit_level)
        upper_side = position // half_span % 2 == 1
        phases = (position % half_span).astype(jnp.float32) * (-math.pi / half_span)
        diff_re, diff_im = split_halves(partner - signal)
        turned_re, turned_im = rotate(diff_re, diff_im, jnp.cos(phases), jnp.sin(phases))
        signal = jnp.where(upper_side, join_halves(turned_re, turned_im), signal + partner)
    return signal


def inverse_sections(signal):
    position = lax.axis_index("seq")
    sections = section_count()
    for bit_level in range(sections):
        half_span = 1 << bit_level
        partner = partner_2(signal, "seq", bit_level)
        upper_side = position // half_span % 2 == 1
        phases = (position % half_span).astype(jnp.float32) * (math.pi / half_span)
        source = jnp.where(upper_side, signal, partner)
        base_term = jnp.where(upper_side, partner, signal)
        source_re, source_im = split_halves(source)
        turned_re, turned_im = rotate(source_re, source_im, jnp.cos(phases), jnp.sin(phases))
        turned = join_halves(turned_re, turned_im)
        signal = 0.5 * jnp.where(upper_side, base_term - turned, base_term + turned)
    return signal


def forward_dft(signal, dft_matrix):
    signal = forward_sections(signal)
    signal = inner_twiddle(signal, held_index(), -1.0)
    return jnp.dot(
        signal, dft_matrix, precision=lax.Precision.HIGHEST, preferred_element_type=jnp.float32
    )


def inverse_dft(spectra, dft_matrix):
    signal = jnp.dot(
        spectra, dft_matrix, precision=lax.Precision.HIGHEST, preferred_element_type=jnp.float32
    )
    signal = inner_twiddle(signal, held_index(), 1.0)
    return inverse_sections(signal)


def local(streams, short_filters, long_filter, skip_gain, out_grad):
    tap_count = short_filters.shape[1]
    reach_back = tap_count - 1
    channels_dev = streams.shape[1]
    length = streams.shape[2]
    filters = long_filter.shape[0]
    members = channels_dev // filters
    devices = lax.axis_size("seq")
    position = lax.axis_index("seq")
    seq_total = length * devices
    preceding = shifted(streams[:, :, length - reach_back :], "seq", 1)
    extended = jnp.concatenate([preceding, streams], axis=2).astype(jnp.float32)
    filtered = jnp.zeros(streams.shape, jnp.float32)
    for offset in range(tap_count):
        filtered = (
            filtered
            + short_filters[:, offset, :, None]
            * extended[:, :, reach_back - offset : reach_back - offset + length]
        )
    gate_out = filtered[0]
    gate_in = filtered[1]
    values = filtered[2]
    gated_prod = gate_in * values
    out_float = out_grad.astype(jnp.float32)
    gate_grad = out_float * gate_out
    signals = jnp.concatenate([gated_prod, gate_grad, long_filter], axis=0)
    twist_phase = (position * length + jnp.arange(length, dtype=jnp.int32)).astype(jnp.float32) * (
        -math.pi / seq_total
    )
    twist_re = jnp.cos(twist_phase)
    twist_im = jnp.sin(twist_phase)
    even_part = join_halves(signals, jnp.zeros_like(signals))
    odd_part = join_halves(signals * twist_re, signals * twist_im)
    spectra = forward_dft(
        jnp.concatenate([even_part, odd_part], axis=0), dft_table(length, -1.0, 1.0)
    )
    row_count = signals.shape[0]
    halves = (spectra[:row_count], spectra[row_count:])
    filter_specs = (halves[0][2 * channels_dev :], halves[1][2 * channels_dev :])
    products = []
    for half_index in range(2):
        part_spec = halves[half_index]
        gated_spec = part_spec[:channels_dev]
        grad_spec = part_spec[channels_dev : 2 * channels_dev]
        wide_filter = jnp.tile(filter_specs[half_index], (members, 1))
        products.append(complex_product(gated_spec, wide_filter, False))
        products.append(complex_product(grad_spec, wide_filter, True))
        products.append(
            complex_product(grad_spec, gated_spec, True)
            .reshape(members, filters, 2 * length)
            .sum(axis=0)
        )
    time_rows = inverse_dft(jnp.concatenate(products, axis=0), dft_table(length, 1.0, 1.0 / length))
    part_rows = 2 * channels_dev + filters
    even_re, even_im = split_halves(time_rows[:part_rows])
    odd_re, odd_im = split_halves(time_rows[part_rows:])
    combined = 0.5 * (even_re + twist_re * odd_re + twist_im * odd_im)
    conv_part = combined[:channels_dev]
    corr_part = combined[channels_dev : 2 * channels_dev]
    filter_local = combined[2 * channels_dev :]
    conv_out = conv_part + skip_gain[:, None] * gated_prod
    gated_grad = corr_part + skip_gain[:, None] * gate_grad
    members_total = channels_dev * lax.axis_size("chan") // filters
    filter_grad = lax.psum(filter_local, "chan") * (1.0 / math.sqrt(members_total * seq_total))
    grads_in = jnp.stack([out_float * conv_out, gated_grad * values, gated_grad * gate_in])
    following = shifted(grads_in[:, :, :reach_back], "seq", -1)
    extended_grad = jnp.concatenate([grads_in, following], axis=2)
    result = jnp.zeros(grads_in.shape, jnp.float32)
    for offset in range(tap_count):
        result = (
            result
            + short_filters[:, offset, :, None] * extended_grad[:, :, offset : offset + length]
        )
    return (result.astype(jnp.bfloat16), filter_grad)


def solution(mesh):
    in_specs = (
        P(None, "chan", "seq"),
        P(None, None, "chan"),
        P(None, "seq"),
        P("chan"),
        P("chan", "seq"),
    )
    out_specs = (P(None, "chan", "seq"), P(None, "seq"))
    return jax.shard_map(local, mesh=mesh, in_specs=in_specs, out_specs=out_specs, check_vma=False)
```

profile of v0, /device:TPU:0, one launch (start us, length us, event | category | flops | bytes accessed | tf_op | source)
XLA Modules:
  0.0 611.4 jit_solution(11527315104026521100)
XLA Ops:
  8.4 4.8 collective-permute-start
  17.5 1.9 select_maximum_fusion
  19.4 3.4 collective-permute-start.1
  23.0 100.9 %collective-permute-done.1 = f32[1152,512]{0,1:T(8,128)} collective-permute-done((f32[1152,512]{0,1:T(8,128)}, f32[1152,512]{0,1:T(8,128)}, u32[]{:S(2)}, u32[]{:S(2)}) %collective-permute-start.1) | collective-permute-done | bytes 2359328 | tf_op jit(solution)/shard_map/ppermute | solution.py:12
  123.9 2.1 fusion.50
  126.3 2.5 maximum_select_fusion
  129.7 51.3 %collective-permute-done.2 = f32[1152,512]{0,1:T(8,128)} collective-permute-done((f32[1152,512]{0,1:T(8,128)S(1)}, f32[1152,512]{0,1:T(8,128)}, u32[]{:S(2)}, u32[]{:S(2)}) %collective-permute-start.2) | collective-permute-done | bytes 2359328 | tf_op jit(solution)/shard_map/ppermute | solution.py:12
  181.0 1.9 sub.100
  183.2 3.5 maximum_select_fusion.1
  188.4 50.0 %collective-permute-done.3 = f32[1152,512]{0,1:T(8,128)S(1)} collective-permute-done((f32[1152,512]{0,1:T(8,128)}, f32[1152,512]{0,1:T(8,128)S(1)}, u32[]{:S(2)}, u32[]{:S(2)}) %collective-permute-start.3) | collective-permute-done | bytes 2359328 | tf_op jit(solution)/shard_map/ppermute | solution.py:12
  238.4 2.8 sub.102
  241.4 2.8 maximum_select_fusion.2
  247.5 1.7 fusion.43
  250.2 1.8 sine_multiply_fusion
  252.0 42.9 %collective-permute-done.4 = f32[1152,512]{0,1:T(8,128)} collective-permute-done((f32[1152,512]{0,1:T(8,128)S(1)}, f32[1152,512]{0,1:T(8,128)}, u32[]{:S(2)}, u32[]{:S(2)}) %collective-permute-start.4) | collective-permute-done | bytes 2359328 | tf_op jit(solution)/shard_map/ppermute | solution.py:12
  295.0 1.9 sub.104
  297.0 2.1 maximum_select_fusion.3
  299.5 4.0 fusion
  309.7 4.8 fusion.11
  316.6 48.1 %collective-permute-done.5 = f32[1152,512]{0,1:T(8,128)S(1)} collective-permute-done((f32[1152,512]{0,1:T(8,128)S(1)}, f32[1152,512]{0,1:T(8,128)S(1)}, u32[]{:S(2)}, u32[]{:S(2)}) %collective-permute-start.5) | collective-permute-done | bytes 2359328 | tf_op jit(solution)/shard_map/ppermute | solution.py:12
  365.8 1.6 collective-permute-start.6
  367.5 47.1 %collective-permute-done.6 = f32[1152,512]{0,1:T(8,128)} collective-permute-done((f32[1152,512]{0,1:T(8,128)S(1)}, f32[1152,512]{0,1:T(8,128)}, u32[]{:S(2)}, u32[]{:S(2)}) %collective-permute-start.6) | collective-permute-done | bytes 2359328 | tf_op jit(solution)/shard_map/ppermute | solution.py:12
  414.6 1.9 broadcast_select_fusion.1
  416.8 1.8 select_multiply_fusion.2
  418.6 5.1 collective-permute-start.7
  423.9 46.9 %collective-permute-done.7 = f32[1152,512]{0,1:T(8,128)S(1)} collective-permute-done((f32[1152,512]{0,1:T(8,128)}, f32[1152,512]{0,1:T(8,128)S(1)}, u32[]{:S(2)}, u32[]{:S(2)}) %collective-permute-start.7) | collective-permute-done | bytes 2359328 | tf_op jit(solution)/shard_map/ppermute | solution.py:12
  472.6 2.1 select_multiply_fusion.1
  474.6 5.0 collective-permute-start.8
  479.8 96.8 %collective-permute-done.8 = f32[1152,512]{0,1:T(8,128)} collective-permute-done((f32[1152,512]{0,1:T(8,128)S(1)}, f32[1152,512]{0,1:T(8,128)}, u32[]{:S(2)}, u32[]{:S(2)}) %collective-permute-start.8) | collective-permute-done | bytes 2359328 | tf_op jit(solution)/shard_map/ppermute | solution.py:12
  576.6 1.9 broadcast_select_fusion.3
  582.8 3.7 collective-permute-done.9
  588.2 14.7 %all-reduce.3.cloned.1.call-done = f32[64,256]{0,1:T(8,128)} async-done(((f32[64,256]{0,1:T(8,128)}), f32[64,256]{0,1:T(8,128)}) %all-reduce.3.cloned.1.call-update) | async-done | bytes 65552 | tf_op jit(solution)/shard_map/psum | solution.py:193
  (127 shorter events, 31.5 us)
Async XLA Ops:
  7.2 595.8 %all-reduce.3.cloned.1.call-start = ((), (), s32[]{:S(2)}) async-start(), calls=%async_computation | async-start | bytes 262144 | tf_op jit(solution)/shard_map/psum | solution.py:193
  8.4 8.0 %collective-permute-start = (bf16[3,256,6]{1,2,0:T(8,128)(2,1)S(1)}, bf16[3,256,6]{1,2,0:T(8,128)(2,1)S(1)}, u32[]{:S(2)}, u32[]{:S(2)}) collective-permute-start(bf16[3,256,6]{1,2,0:T(8,128)(2,1)S(1)} %slice.304), channel_id=1, source_target_pairs={{0,2},{2,4},{4,6},{6,8},{8,10},{10,12},{12,14},{14,16},{16,18},{18... | collective-permute-start | bytes 27656 | tf_op jit(solution)/shard_map/ppermute | solution.py:18
  14.3 2.9 copy-start.17
  14.3 2.9 copy-start.19
  14.4 2.9 copy-start.23
  14.4 2.9 copy-start.25
  14.4 2.8 copy-start.21
  15.4 1.8 copy-start.6
  17.2 2.2 copy-start.4
  17.5 108.5 %copy-start = (f32[576,256]{0,1:T(8,128)}, f32[576,256]{0,1:T(8,128)S(1)}, u32[]{:S(2)}) copy-start(f32[576,256]{0,1:T(8,128)S(1)} %get-tuple-element.46) | copy-start | bytes 1769476
  17.5 108.5 %copy-start.1 = (f32[576,256]{0,1:T(8,128)}, f32[576,256]{0,1:T(8,128)S(1)}, u32[]{:S(2)}) copy-start(f32[576,256]{0,1:T(8,128)S(1)} %get-tuple-element.47) | copy-start | bytes 1769476
  19.4 104.5 %collective-permute-start.1 = (f32[1152,512]{0,1:T(8,128)}, f32[1152,512]{0,1:T(8,128)}, u32[]{:S(2)}, u32[]{:S(2)}) collective-permute-start(f32[1152,512]{0,1:T(8,128)} %select_maximum_fusion), channel_id=1, source_target_pairs={{0,16},{2,18},{4,20},{6,22},{8,24},{10,26},{12,28},{14,30},{16,0},... | collective-permute-start | bytes 7077896 | tf_op jit(solution)/shard_map/ppermute | solution.py:12
  128.8 52.3 %collective-permute-start.2 = (f32[1152,512]{0,1:T(8,128)S(1)}, f32[1152,512]{0,1:T(8,128)}, u32[]{:S(2)}, u32[]{:S(2)}) collective-permute-start(f32[1152,512]{0,1:T(8,128)S(1)} %maximum_select_fusion), channel_id=1, source_target_pairs={{0,8},{2,10},{4,12},{6,14},{8,0},{10,2},{12,4},{14,6},{16,24},{18,... | collective-permute-start | bytes 7077896 | tf_op jit(solution)/shard_map/ppermute | solution.py:12
  186.7 51.7 %collective-permute-start.3 = (f32[1152,512]{0,1:T(8,128)}, f32[1152,512]{0,1:T(8,128)S(1)}, u32[]{:S(2)}, u32[]{:S(2)}) collective-permute-start(f32[1152,512]{0,1:T(8,128)} %maximum_select_fusion.1), channel_id=1, source_target_pairs={{0,4},{2,6},{4,0},{6,2},{8,12},{10,14},{12,8},{14,10},{16,20},{18,... | collective-permute-start | bytes 7077896 | tf_op jit(solution)/shard_map/ppermute | solution.py:12
  238.4 2.8 copy-start.2
  244.2 50.7 %collective-permute-start.4 = (f32[1152,512]{0,1:T(8,128)S(1)}, f32[1152,512]{0,1:T(8,128)}, u32[]{:S(2)}, u32[]{:S(2)}) collective-permute-start(f32[1152,512]{0,1:T(8,128)S(1)} %maximum_select_fusion.2), channel_id=1, source_target_pairs={{0,2},{2,0},{4,6},{6,4},{8,10},{10,8},{12,14},{14,12},{16,18},{18,... | collective-permute-start | bytes 7077896 | tf_op jit(solution)/shard_map/ppermute | solution.py:12
  308.3 1.2 copy-start.15
  308.3 1.2 copy-start.12
  308.3 1.3 copy-start.13
  308.3 1.4 copy-start.14
  309.7 4.8 copy-start.27
  309.7 4.8 copy-start.28
  315.0 49.7 %collective-permute-start.5 = (f32[1152,512]{0,1:T(8,128)S(1)}, f32[1152,512]{0,1:T(8,128)S(1)}, u32[]{:S(2)}, u32[]{:S(2)}) collective-permute-start(f32[1152,512]{0,1:T(8,128)S(1)} %pad_maximum_fusion), channel_id=1, source_target_pairs={{0,2},{2,0},{4,6},{6,4},{8,10},{10,8},{12,14},{14,12},{16,18},{18,... | collective-permute-start | bytes 7077896 | tf_op jit(solution)/shard_map/ppermute | solution.py:12
  365.8 48.9 %collective-permute-start.6 = (f32[1152,512]{0,1:T(8,128)S(1)}, f32[1152,512]{0,1:T(8,128)}, u32[]{:S(2)}, u32[]{:S(2)}) collective-permute-start(f32[1152,512]{0,1:T(8,128)S(1)} %select_multiply_fusion.3), channel_id=1, source_target_pairs={{0,4},{2,6},{4,0},{6,2},{8,12},{10,14},{12,8},{14,10},{16,20},{18,... | collective-permute-start | bytes 7077896 | tf_op jit(solution)/shard_map/ppermute | solution.py:12
  418.6 52.2 %collective-permute-start.7 = (f32[1152,512]{0,1:T(8,128)}, f32[1152,512]{0,1:T(8,128)S(1)}, u32[]{:S(2)}, u32[]{:S(2)}) collective-permute-start(f32[1152,512]{0,1:T(8,128)} %select_multiply_fusion.2), channel_id=1, source_target_pairs={{0,8},{2,10},{4,12},{6,14},{8,0},{10,2},{12,4},{14,6},{16,24},{18,... | collective-permute-start | bytes 7077896 | tf_op jit(solution)/shard_map/ppermute | solution.py:12
  470.8 1.5 copy-start.3
  474.6 102.0 %collective-permute-start.8 = (f32[1152,512]{0,1:T(8,128)S(1)}, f32[1152,512]{0,1:T(8,128)}, u32[]{:S(2)}, u32[]{:S(2)}) collective-permute-start(f32[1152,512]{0,1:T(8,128)S(1)} %select_multiply_fusion.1), channel_id=1, source_target_pairs={{0,16},{2,18},{4,20},{6,22},{8,24},{10,26},{12,28},{14,30},{16,0},... | collective-permute-start | bytes 7077896 | tf_op jit(solution)/shard_map/ppermute | solution.py:12
  579.5 1.1 copy-start.29
  580.7 5.9 copy-start.18
  580.7 5.9 copy-start.20
  580.7 5.9 copy-start.22
  580.8 5.7 collective-permute-start.9
  (9 other events, 8.8 us)
Sparse Core Ops, SparseCore 0:
  582.9 19.9 all-reduce.2
where the time goes:
time: 612 us; the launch traced here: 611 us
  waiting for transfers between devices  503 us (82%)
  other arithmetic  47.7 us (8%)
  starting transfers between devices  26.7 us (4%)
  between operations  15.8 us (3%)
  local copies, waits for them, and re-layouts  9.85 us (2%)
  matrix products  8.79 us (1%)
    ppermute x8, waiting for transfers between devices, partner_2(): return lax.ppermute(value, axis, pairs)  484 us
    ppermute x8, starting transfers between devices, partner_2(): return lax.ppermute(value, axis, pairs)  20.5 us
    psum x1, waiting for transfers between devices, local(): lax.psum(filter_local, 'chan')  14.7 us
  transfers between devices with their start and end apart: 11, of which 10 were waited for; matrix products, arithmetic and copies ran while one was open for 2% of the time, Pallas kernels for 0%

commit v1 on v0

--- a/solution.py
+++ b/solution.py
@@ -1,9 +1,16 @@
+import functools
 import math
 
 import jax
 import jax.numpy as jnp
+import ml_dtypes
+import numpy as np
 from jax import lax
+from jax.experimental import pallas as pl
+from jax.experimental.pallas import tpu as pltpu
 from jax.sharding import PartitionSpec as P
+
+MESH = pl.DeviceIdType.MESH
 
 
 def partner_2(value, axis, apart):
@@ -203,6 +210,454 @@
     return (result.astype(jnp.bfloat16), filter_grad)
 
 
+BF16 = jnp.bfloat16
+F32 = jnp.float32
+LANES = 128
+
+
+def split16(value):
+    high = value.astype(BF16)
+    return high, (value - high.astype(F32)).astype(BF16)
+
+
+def host_split(table):
+    high = table.astype(np.float32).astype(ml_dtypes.bfloat16)
+    low = (table - high.astype(np.float64)).astype(np.float32).astype(ml_dtypes.bfloat16)
+    return high, low
+
+
+def one_hot_rows(sources):
+    table = np.zeros((len(sources), len(sources)), np.float32)
+    table[np.arange(len(sources)), sources] = 1.0
+    return table.astype(ml_dtypes.bfloat16)
+
+
+def tables(channels, filters, devices, tokens):
+    members = channels // filters
+    own_filters = filters // devices
+    rows = np.arange(channels)
+    order = one_hot_rows(filters * (rows % members) + rows // members)
+    rows = np.arange(4 * filters)
+    owner, kind, own = rows // (4 * own_filters), rows // own_filters % 4, rows % own_filters
+    filter_order = one_hot_rows(kind * filters + owner * own_filters + own)
+    fft_size = 2 * tokens
+    outer = fft_size // LANES
+    used = outer // 2
+    angle = 2.0 * math.pi * (np.outer(np.arange(outer), np.arange(used)) % outer) / outer
+    cosine, sine = np.cos(angle), np.sin(angle)
+    first = np.block([[cosine, sine], [-sine, cosine]])
+    high, low = host_split(first)
+    first_cat = np.concatenate([high, low, high], axis=1)
+    high, low = high[:, :used], low[:, :used]
+    first_real = np.concatenate([high, low, high], axis=1)
+    last = np.block([[cosine.T, -sine.T], [sine.T, cosine.T]]) / fft_size
+    high, low = host_split(last)
+    last_cat = np.concatenate([high, low, high], axis=1)
+    angle = 2.0 * math.pi * (np.outer(np.arange(LANES), np.arange(LANES)) % LANES) / LANES
+    cosine, sine = np.cos(angle), np.sin(angle)
+    inner = np.stack(host_split(np.block([[cosine, -sine], [sine, cosine]])))
+    inner_back = np.stack(host_split(np.block([[cosine, sine], [-sine, cosine]])))
+    angle = -2.0 * math.pi * np.outer(np.arange(outer), np.arange(LANES)) / fft_size
+    twiddles = np.stack([np.cos(angle), np.sin(angle)]).astype(np.float32)
+    return (
+        order,
+        np.ascontiguousarray(order.T),
+        filter_order,
+        np.ascontiguousarray(filter_order.T),
+        first_cat,
+        first_real,
+        last_cat,
+        inner,
+        inner_back,
+        twiddles,
+    )
+
+
+def dot32(left, right):
+    return jnp.dot(left, right, preferred_element_type=F32)
+
+
+def inner_product(value, table_ref):
+    high, low = split16(value)
+    return dot32(high, table_ref[0]) + dot32(low, table_ref[0]) + dot32(high, table_ref[1])
+
+
+def outer_product(table, value):
+    high, low = split16(value)
+    return dot32(table, jnp.concatenate([high, high, low], axis=0))
+
+
+def halves_of(value):
+    return value[:, :LANES], value[:, LANES:]
+
+
+def product(first, second, conjugate):
+    a, b = halves_of(first)
+    c, d = halves_of(second)
+    if conjugate:
+        return jnp.concatenate([a * c + b * d, b * c - a * d], axis=1)
+    return jnp.concatenate([a * c - b * d, a * d + b * c], axis=1)
+
+
+def delayed(value, by):
+    if by == 0:
+        return value
+    zeros = jnp.zeros((value.shape[0], LANES), F32)
+    return pltpu.roll(jnp.concatenate([zeros, value], axis=1), by, 1)[:, LANES:]
+
+
+def advanced(value, by):
+    if by == 0:
+        return value
+    length = value.shape[1]
+    zeros = jnp.zeros((value.shape[0], LANES), F32)
+    return pltpu.roll(jnp.concatenate([value, zeros], axis=1), length + LANES - by, 1)[:, :length]
+
+
+def kernel(
+    filter_scale,
+    streams,
+    out_grad,
+    long_filter,
+    short_filters,
+    skip_gain,
+    order,
+    order_t,
+    filter_order,
+    filter_order_t,
+    first_cat,
+    first_real,
+    last_cat,
+    inner,
+    inner_back,
+    twiddles,
+    stream_grad,
+    filter_grad,
+    sent,
+    held,
+    answers,
+    results,
+    signal_rows,
+    filter_rows,
+    own_part,
+    other_part,
+    send_sem,
+    recv_sem,
+    back_send_sem,
+    back_recv_sem,
+    part_sem,
+):
+    devices = sent.shape[0]
+    rows = sent.shape[1]
+    length = streams.shape[2]
+    filters = long_filter.shape[0]
+    taps = short_filters.shape[1]
+    own_filters = filters // devices
+    members = rows // own_filters
+    pairs = rows // 2
+    per_filter = members // 2
+    used = devices * length // LANES
+    outer = 2 * used
+    pieces = length // LANES
+    me = lax.axis_index("seq")
+    other = 1 - lax.axis_index("chan")
+
+    barrier = pltpu.get_barrier_semaphore()
+    for step in range(1, devices):
+        pl.semaphore_signal(
+            barrier, inc=1, device_id={"seq": lax.rem(me + step, devices)}, device_id_type=MESH
+        )
+    pl.semaphore_signal(barrier, inc=1, device_id={"chan": other}, device_id_type=MESH)
+
+    for index in range(4):
+        block = out_grad[...] if index == 3 else streams[index]
+        moved = dot32(order[...], block).astype(BF16)
+        sent[:, :, index * length : (index + 1) * length] = moved.reshape(devices, rows, length)
+    high, low = split16(long_filter[...])
+    stacked = []
+    for piece in range(pieces):
+        columns = slice(piece * LANES, (piece + 1) * LANES)
+        stacked += [high[:, columns], low[:, columns]]
+    moved = dot32(filter_order[...], jnp.concatenate(stacked, axis=0)).astype(BF16)
+    sent[:, :, 4 * length :] = moved.reshape(devices, rows, LANES)
+
+    pl.semaphore_wait(barrier, devices)
+
+    def exchange(source, target, send, recv):
+        copies = []
+        for step in range(1, devices):
+            peer = lax.rem(me + step, devices)
+            copy = pltpu.make_async_remote_copy(
+                src_ref=source.at[peer],
+                dst_ref=target.at[me],
+                send_sem=send.at[peer],
+                recv_sem=recv.at[me],
+                device_id={"seq": peer},
+                device_id_type=MESH,
+            )
+            copy.start()
+            copies.append(copy)
+        target[me] = source[me]
+        return copies
+
+    def finish(copies, source, target, send, recv):
+        for step in range(1, devices):
+            peer = lax.rem(me + step, devices)
+            pltpu.make_async_remote_copy(
+                src_ref=source.at[peer],
+                dst_ref=target.at[peer],
+                send_sem=send.at[peer],
+                recv_sem=recv.at[peer],
+                device_id={"seq": peer},
+                device_id_type=MESH,
+            ).wait_recv()
+
+    copies = exchange(sent, held, send_sem, recv_sem)
+    picked = order[pl.ds(pl.multiple_of(me * rows, rows), rows), :].astype(F32)
+
+    def own_columns(values):
+        return lax.dot_general(
+            picked,
+            values,
+            (((1,), (1,)), ((), ())),
+            precision=lax.Precision.HIGHEST,
+            preferred_element_type=F32,
+        )
+
+    weights = [own_columns(short_filters[index]) for index in range(3)]
+    gain = jnp.sum(picked * skip_gain[...], axis=1, keepdims=True)
+    finish(copies, sent, held, send_sem, recv_sem)
+
+    def whole(index):
+        columns = slice(index * length, (index + 1) * length)
+        return jnp.concatenate(
+            [held[source, :, columns].astype(F32) for source in range(devices)], axis=1
+        )
+
+    filtered = []
+    for index in range(3):
+        value = whole(index)
+        total = weights[index][:, 0:1] * value
+        for offset in range(1, taps):
+            total = total + weights[index][:, offset : offset + 1] * delayed(value, offset)
+        filtered.append(total)
+    out_float = whole(3)
+    gated_prod = filtered[1] * filtered[2]
+    gate_grad = out_float * filtered[0]
+    for block in range(used):
+        columns = slice(block * LANES, (block + 1) * LANES)
+        signal_rows[0, block * rows : (block + 1) * rows, :] = gated_prod[:, columns]
+        signal_rows[1, block * rows : (block + 1) * rows, :] = gate_grad[:, columns]
+    for source in range(devices):
+        filter_rows[source * rows : (source + 1) * rows, :] = held[source, :, 4 * length :].astype(
+            F32
+        )
+
+    def channel_rows(which, channel):
+        return signal_rows[which, pl.ds(channel, used, stride=rows), :]
+
+    stride = 2 * own_filters
+
+    def filter_part(part):
+        return jnp.concatenate(
+            [
+                filter_rows[pl.ds(part * own_filters + own, used, stride=stride), :]
+                for own in range(own_filters)
+            ],
+            axis=1,
+        ).astype(BF16)
+
+    def packed(which, part):
+        return [channel_rows(which, 2 * pair + part) for pair in range(pairs)]
+
+    signals = jnp.concatenate(
+        [
+            jnp.concatenate(packed(0, part) + packed(1, part), axis=1)
+            for part in range(2)
+        ],
+        axis=0,
+    )
+    part_high, part_low = filter_part(0), filter_part(1)
+    outer_out = jnp.concatenate(
+        [
+            outer_product(first_cat[...], signals),
+            dot32(first_real[...], jnp.concatenate([part_high, part_high, part_low], axis=0)),
+        ],
+        axis=1,
+    )
+    twiddle_re, twiddle_im = twiddles[0], twiddles[1]
+    count = 2 * pairs + own_filters
+    turned = []
+    for index in range(count):
+        columns = slice(index * LANES, (index + 1) * LANES)
+        real_part, imag_part = outer_out[:outer, columns], outer_out[outer:, columns]
+        turned.append(
+            jnp.concatenate(
+                [
+                    real_part * twiddle_re - imag_part * twiddle_im,
+                    real_part * twiddle_im + imag_part * twiddle_re,
+                ],
+                axis=1,
+            )
+        )
+    spectra = inner_product(jnp.concatenate(turned, axis=0), inner)
+
+    def spectrum(index):
+        return spectra[index * outer : (index + 1) * outer]
+
+    def inverse(values, table):
+        inner_out = inner_product(jnp.concatenate(values, axis=0), inner_back)
+        columns = []
+        for index in range(len(values)):
+            real_part, imag_part = halves_of(inner_out[index * outer : (index + 1) * outer])
+            columns.append(
+                jnp.concatenate(
+                    [
+                        real_part * twiddle_re + imag_part * twiddle_im,
+                        imag_part * twiddle_re - real_part * twiddle_im,
+                    ],
+                    axis=0,
+                )
+            )
+        return outer_product(table, jnp.concatenate(columns, axis=1))
+
+    sums = []
+    for own in range(own_filters):
+        total = None
+        for index in range(own * per_filter, (own + 1) * per_filter):
+            term = product(spectrum(pairs + index), spectrum(index), True)
+            total = term if total is None else total + term
+        sums.append(total)
+    own_part[...] = inverse(sums, last_cat[:used, :])
+    part_copy = pltpu.make_async_remote_copy(
+        src_ref=own_part,
+        dst_ref=other_part,
+        send_sem=part_sem.at[0],
+        recv_sem=part_sem.at[1],
+        device_id={"chan": other},
+        device_id_type=MESH,
+    )
+    part_copy.start()
+
+    products = []
+    for index in range(2 * pairs):
+        filter_spec = spectrum(2 * pairs + index % pairs // per_filter)
+        products.append(product(spectrum(index), filter_spec, index >= pairs))
+    times = inverse(products, last_cat[...])
+    for index in range(2 * pairs):
+        which, pair = index // pairs, index % pairs
+        columns = slice(index * LANES, (index + 1) * LANES)
+        for part in range(2):
+            signal_rows[which, pl.ds(2 * pair + part, used, stride=rows), :] = times[
+                part * used : (part + 1) * used, columns
+            ]
+
+    def joined(which):
+        return jnp.concatenate(
+            [signal_rows[which, block * rows : (block + 1) * rows, :] for block in range(used)],
+            axis=1,
+        )
+
+    conv_out = joined(0) + gain * gated_prod
+    gated_grad = joined(1) + gain * gate_grad
+    grads = (out_float * conv_out, gated_grad * filtered[2], gated_grad * filtered[1])
+    for index in range(3):
+        value = grads[index]
+        total = weights[index][:, 0:1] * value
+        for offset in range(1, taps):
+            total = total + weights[index][:, offset : offset + 1] * advanced(value, offset)
+        total = total.astype(BF16)
+        for target in range(devices):
+            answers[target, :, index * length : (index + 1) * length] = total[
+                :, target * length : (target + 1) * length
+            ]
+
+    part_copy.wait()
+    high, low = split16((own_part[...] + other_part[...]) * filter_scale)
+    for own in range(own_filters):
+        columns = slice(own * LANES, (own + 1) * LANES)
+        filter_rows[pl.ds(own, used, stride=stride), :] = high[:, columns].astype(F32)
+        filter_rows[pl.ds(own_filters + own, used, stride=stride), :] = low[:, columns].astype(F32)
+    for target in range(devices):
+        answers[target, :, 3 * length :] = filter_rows[
+            target * rows : (target + 1) * rows, :
+        ].astype(BF16)
+
+    back_copies = exchange(answers, results, back_send_sem, back_recv_sem)
+    for copy in copies:
+        copy.wait_send()
+    finish(back_copies, answers, results, back_send_sem, back_recv_sem)
+    for index in range(3):
+        block = results[:, :, index * length : (index + 1) * length].reshape(devices * rows, length)
+        stream_grad[index] = dot32(order_t[...], block).astype(BF16)
+    block = results[:, :, 3 * length :].reshape(devices * rows, LANES)
+    moved = dot32(filter_order_t[...], block)
+    for piece in range(pieces):
+        start = 2 * piece * filters
+        filter_grad[:, piece * LANES : (piece + 1) * LANES] = (
+            moved[start : start + filters] + moved[start + filters : start + 2 * filters]
+        )
+    for copy in back_copies:
+        copy.wait_send()
+
+
+def fast_local(streams, short_filters, long_filter, skip_gain, out_grad):
+    devices = lax.axis_size("seq")
+    channels, length = streams.shape[1:]
+    filters = long_filter.shape[0]
+    tokens = devices * length
+    rows = channels // devices
+    own_filters = filters // devices
+    used = tokens // LANES
+    members_total = channels * lax.axis_size("chan") // filters
+    constants = [jnp.asarray(table) for table in tables(channels, filters, devices, tokens)]
+    arguments = [
+        streams,
+        out_grad,
+        long_filter,
+        short_filters,
+        skip_gain.reshape(1, channels),
+    ] + constants
+    vmem = pl.BlockSpec(memory_space=pltpu.VMEM)
+    width = 4 * length + LANES
+    width_back = 3 * length + LANES
+    return pl.pallas_call(
+        functools.partial(kernel, 1.0 / math.sqrt(members_total * tokens)),
+        out_shape=(
+            jax.ShapeDtypeStruct(streams.shape, BF16),
+            jax.ShapeDtypeStruct(long_filter.shape, F32),
+        ),
+        in_specs=[vmem] * len(arguments),
+        out_specs=(vmem, vmem),
+        scratch_shapes=[
+            pltpu.VMEM((devices, rows, width), BF16),
+            pltpu.VMEM((devices, rows, width), BF16),
+            pltpu.VMEM((devices, rows, width_back), BF16),
+            pltpu.VMEM((devices, rows, width_back), BF16),
+            pltpu.VMEM((2, used * rows, LANES), F32),
+            pltpu.VMEM((devices * rows, LANES), F32),
+            pltpu.VMEM((used, own_filters * LANES), F32),
+            pltpu.VMEM((used, own_filters * LANES), F32),
+            pltpu.SemaphoreType.DMA((devices,)),
+            pltpu.SemaphoreType.DMA((devices,)),
+            pltpu.SemaphoreType.DMA((devices,)),
+            pltpu.SemaphoreType.DMA((devices,)),
+            pltpu.SemaphoreType.DMA((2,)),
+        ],
+        compiler_params=pltpu.CompilerParams(
+            collective_id=0, has_side_effects=True, vmem_limit_bytes=48 * 2**20
+        ),
+    )(*arguments)
+
+
+def fits_fast(mesh, channels, tokens, filters):
+    devices, groups = mesh.shape["seq"], mesh.shape["chan"]
+    channels, length = channels // groups, tokens // devices
+    if groups != 2 or filters % devices or channels % (2 * filters) or channels % (16 * devices):
+        return False
+    return length == 2 * LANES and channels // devices == 4 * (filters // devices)
+
+
 def solution(mesh):
     in_specs = (
         P(None, "chan", "seq"),
@@ -212,4 +667,15 @@
         P("chan", "seq"),
     )
     out_specs = (P(None, "chan", "seq"), P(None, "seq"))
-    return jax.shard_map(local, mesh=mesh, in_specs=in_specs, out_specs=out_specs, check_vma=False)
+
+    def whole_program(streams, short_filters, long_filter, skip_gain, out_grad):
+        fast = fits_fast(mesh, streams.shape[1], streams.shape[2], long_filter.shape[0])
+        return jax.shard_map(
+            fast_local if fast else local,
+            mesh=mesh,
+            in_specs=in_specs,
+            out_specs=out_specs,
+            check_vma=False,
+        )(streams, short_filters, long_filter, skip_gain, out_grad)
+
+    return whole_program

time: 612 us -> 51.2 us (0.08)
  the two profiles are of different devices: /device:TPU:0 before, /device:TPU:28 now
where the time goes in v1:
time: 51.2 us; the launch traced here: 50.6 us
  Pallas kernels  35.7 us (70%)
  local copies, waits for them, and re-layouts  14.3 us (28%)
  between operations  0.66 us (1%)
    pallas_call x1, Pallas kernels, fast_local(): pl.pallas_call(functools.partial(kernel, 1.0 / math.sqrt(members_total *...  35.7 us
    unnamed x32, local copies, waits for them, and re-layouts  14.3 us

profile of v1, /device:TPU:28, one launch (start us, length us, event | category | flops | bytes accessed | tf_op | source)
XLA Modules:
  0.0 50.6 jit_solution(15471213736068591327)
XLA Ops:
  0.6 0.0 copy-start.14
  0.6 0.7 %copy-done.14 = f32[256]{0:T(256)S(1)} copy-done((f32[256]{0:T(256)S(1)}, f32[256]{0:T(256)}, u32[]{:S(2)}) %copy-start.14) | copy-done | bytes 1048
  1.3 0.0 copy-start
  1.3 1.0 %copy-done = bf16[3,256,256]{2,1,0:T(8,128)(2,1)S(1)} copy-done((bf16[3,256,256]{2,1,0:T(8,128)(2,1)S(1)}, bf16[3,256,256]{2,1,0:T(8,128)(2,1)}, u32[]{:S(2)}) %copy-start) | copy-done | bytes 393240
  2.3 0.0 copy-start.1
  2.3 0.9 %copy-done.1 = bf16[2,256,256]{2,1,0:T(8,128)(2,1)S(1)} copy-done((bf16[2,256,256]{2,1,0:T(8,128)(2,1)S(1)}, bf16[2,256,256]{2,1,0:T(8,128)(2,1)}, u32[]{:S(2)}) %copy-start.1) | copy-done | bytes 262168
  3.3 0.0 copy-start.2
  3.3 0.9 %copy-done.2 = bf16[2,256,256]{2,1,0:T(8,128)(2,1)S(1)} copy-done((bf16[2,256,256]{2,1,0:T(8,128)(2,1)S(1)}, bf16[2,256,256]{2,1,0:T(8,128)(2,1)}, u32[]{:S(2)}) %copy-start.2) | copy-done | bytes 262168
  4.2 0.0 copy-start.3
  4.2 0.9 %copy-done.3 = bf16[256,256]{1,0:T(8,128)(2,1)S(1)} copy-done((bf16[256,256]{1,0:T(8,128)(2,1)S(1)}, bf16[256,256]{1,0:T(8,128)(2,1)}, u32[]{:S(2)}) %copy-start.3) | copy-done | bytes 131096
  5.1 0.0 copy-start.4
  5.1 0.9 %copy-done.4 = bf16[256,256]{1,0:T(8,128)(2,1)S(1)} copy-done((bf16[256,256]{1,0:T(8,128)(2,1)S(1)}, bf16[256,256]{1,0:T(8,128)(2,1)}, u32[]{:S(2)}) %copy-start.4) | copy-done | bytes 131096
  6.0 0.0 copy-start.5
  6.0 0.9 %copy-done.5 = bf16[256,256]{1,0:T(8,128)(2,1)S(1)} copy-done((bf16[256,256]{1,0:T(8,128)(2,1)S(1)}, bf16[256,256]{1,0:T(8,128)(2,1)}, u32[]{:S(2)}) %copy-start.5) | copy-done | bytes 131096
  6.9 0.0 copy-start.6
  6.9 0.9 %copy-done.6 = bf16[256,256]{1,0:T(8,128)(2,1)S(1)} copy-done((bf16[256,256]{1,0:T(8,128)(2,1)S(1)}, bf16[256,256]{1,0:T(8,128)(2,1)}, u32[]{:S(2)}) %copy-start.6) | copy-done | bytes 131096
  7.8 0.9 %copy-done.7 = bf16[256,256]{1,0:T(8,128)(2,1)S(1)} copy-done((bf16[256,256]{1,0:T(8,128)(2,1)S(1)}, bf16[256,256]{1,0:T(8,128)(2,1)}, u32[]{:S(2)}) %copy-start.7) | copy-done | bytes 131096
  8.7 0.0 copy-start.8
  8.7 0.8 %copy-done.8 = f32[64,256]{1,0:T(8,128)S(1)} copy-done((f32[64,256]{1,0:T(8,128)S(1)}, f32[64,256]{1,0:T(8,128)}, u32[]{:S(2)}) %copy-start.8) | copy-done | bytes 65560
  9.6 0.0 copy-start.9
  9.6 0.8 %copy-done.9 = f32[2,64,128]{2,1,0:T(8,128)S(1)} copy-done((f32[2,64,128]{2,1,0:T(8,128)S(1)}, f32[2,64,128]{2,1,0:T(8,128)}, u32[]{:S(2)}) %copy-start.9) | copy-done | bytes 65560
  10.4 0.0 copy-start.10
  10.4 0.8 %copy-done.10 = bf16[128,192]{1,0:T(8,128)(2,1)S(1)} copy-done((bf16[128,192]{1,0:T(8,128)(2,1)S(1)}, bf16[128,192]{1,0:T(8,128)(2,1)}, u32[]{:S(2)}) %copy-start.10) | copy-done | bytes 49176
  11.3 0.0 copy-start.11
  11.3 0.8 %copy-done.11 = bf16[64,384]{1,0:T(8,128)(2,1)S(1)} copy-done((bf16[64,384]{1,0:T(8,128)(2,1)S(1)}, bf16[64,384]{1,0:T(8,128)(2,1)}, u32[]{:S(2)}) %copy-start.11) | copy-done | bytes 49176
  12.1 0.0 copy-start.12
  12.1 0.8 %copy-done.12 = bf16[128,96]{1,0:T(8,128)(2,1)S(1)} copy-done((bf16[128,96]{1,0:T(8,128)(2,1)S(1)}, bf16[128,96]{1,0:T(8,128)(2,1)}, u32[]{:S(2)}) %copy-start.12) | copy-done | bytes 24600
  12.8 0.0 copy-start.13
  12.8 0.7 %copy-done.13 = f32[3,7,256]{2,1,0:T(8,128)S(1)} copy-done((f32[3,7,256]{2,1,0:T(8,128)S(1)}, f32[3,7,256]{2,1,0:T(8,128)}, u32[]{:S(2)}) %copy-start.13) | copy-done | bytes 21528
  13.5 35.7 %shard_map.158 = (bf16[3,256,256]{2,1,0:T(8,128)(2,1)S(1)}, f32[64,256]{1,0:T(8,128)S(1)}) custom-call(bf16[3,256,256]{2,1,0:T(8,128)(2,1)S(1)} %copy-done, bf16[256,256]{1,0:T(8,128)(2,1)S(1)} %copy-done.3, f32[64,256]{1,0:T(8,128)S(1)} %copy-done.8, f32[3,7,256]{2,1,0:T(8,128)S(1)} %copy-done.13, f32[1,256]{1,0:T(1,128)S(1)} %bitcast.1, ...), custom_call_target="tpu_custom_call" | custom-call | tf_op jit(solution)/shard_map/pallas_call | solution.py:624
  49.2 0.7 %copy.19 = bf16[3,256,256]{2,1,0:T(8,128)(2,1)} copy(bf16[3,256,256]{2,1,0:T(8,128)(2,1)S(1)} %get-tuple-element.4) | data formatting | bytes 786432
  50.0 0.6 %copy.20 = f32[64,256]{1,0:T(8,128)} copy(f32[64,256]{1,0:T(8,128)S(1)} %get-tuple-element.5) | data formatting | bytes 131072
  (1 shorter events, 0.0 us)
Async XLA Ops:
  0.6 0.7 %copy-start.14 = (f32[256]{0:T(256)S(1)}, f32[256]{0:T(256)}, u32[]{:S(2)}) copy-start(f32[256]{0:T(256)} %param.18) | copy-start | bytes 3076
  1.3 1.0 %copy-start = (bf16[3,256,256]{2,1,0:T(8,128)(2,1)S(1)}, bf16[3,256,256]{2,1,0:T(8,128)(2,1)}, u32[]{:S(2)}) copy-start(bf16[3,256,256]{2,1,0:T(8,128)(2,1)} %streams.1) | copy-start | bytes 1179652
  2.3 0.9 %copy-start.1 = (bf16[2,256,256]{2,1,0:T(8,128)(2,1)S(1)}, bf16[2,256,256]{2,1,0:T(8,128)(2,1)}, u32[]{:S(2)}) copy-start(bf16[2,256,256]{2,1,0:T(8,128)(2,1)} %constant.28.clone.inner_back) | copy-start | bytes 786436
  3.3 0.9 %copy-start.2 = (bf16[2,256,256]{2,1,0:T(8,128)(2,1)S(1)}, bf16[2,256,256]{2,1,0:T(8,128)(2,1)}, u32[]{:S(2)}) copy-start(bf16[2,256,256]{2,1,0:T(8,128)(2,1)} %constant.27.clone.inner) | copy-start | bytes 786436
  4.2 0.9 %copy-start.3 = (bf16[256,256]{1,0:T(8,128)(2,1)S(1)}, bf16[256,256]{1,0:T(8,128)(2,1)}, u32[]{:S(2)}) copy-start(bf16[256,256]{1,0:T(8,128)(2,1)} %out_grad.1) | copy-start | bytes 393220
  5.1 0.9 %copy-start.4 = (bf16[256,256]{1,0:T(8,128)(2,1)S(1)}, bf16[256,256]{1,0:T(8,128)(2,1)}, u32[]{:S(2)}) copy-start(bf16[256,256]{1,0:T(8,128)(2,1)} %constant.23.clone.filter_order_t) | copy-start | bytes 393220
  6.0 0.9 %copy-start.5 = (bf16[256,256]{1,0:T(8,128)(2,1)S(1)}, bf16[256,256]{1,0:T(8,128)(2,1)}, u32[]{:S(2)}) copy-start(bf16[256,256]{1,0:T(8,128)(2,1)} %constant.22.clone.filter_order) | copy-start | bytes 393220
  6.9 0.9 %copy-start.6 = (bf16[256,256]{1,0:T(8,128)(2,1)S(1)}, bf16[256,256]{1,0:T(8,128)(2,1)}, u32[]{:S(2)}) copy-start(bf16[256,256]{1,0:T(8,128)(2,1)} %constant.21.clone.order_t) | copy-start | bytes 393220
  7.8 0.9 %copy-start.7 = (bf16[256,256]{1,0:T(8,128)(2,1)S(1)}, bf16[256,256]{1,0:T(8,128)(2,1)}, u32[]{:S(2)}) copy-start(bf16[256,256]{1,0:T(8,128)(2,1)} %constant.20.clone.order) | copy-start | bytes 393220
  8.7 0.8 %copy-start.8 = (f32[64,256]{1,0:T(8,128)S(1)}, f32[64,256]{1,0:T(8,128)}, u32[]{:S(2)}) copy-start(f32[64,256]{1,0:T(8,128)} %long_filter.1) | copy-start | bytes 196612
  9.6 0.8 %copy-start.9 = (f32[2,64,128]{2,1,0:T(8,128)S(1)}, f32[2,64,128]{2,1,0:T(8,128)}, u32[]{:S(2)}) copy-start(f32[2,64,128]{2,1,0:T(8,128)} %constant.29.clone.twiddles) | copy-start | bytes 196612
  10.4 0.8 %copy-start.10 = (bf16[128,192]{1,0:T(8,128)(2,1)S(1)}, bf16[128,192]{1,0:T(8,128)(2,1)}, u32[]{:S(2)}) copy-start(bf16[128,192]{1,0:T(8,128)(2,1)} %constant.24.clone.first_cat) | copy-start | bytes 147460
  11.3 0.8 %copy-start.11 = (bf16[64,384]{1,0:T(8,128)(2,1)S(1)}, bf16[64,384]{1,0:T(8,128)(2,1)}, u32[]{:S(2)}) copy-start(bf16[64,384]{1,0:T(8,128)(2,1)} %constant.26.clone.last_cat) | copy-start | bytes 147460
  12.1 0.8 %copy-start.12 = (bf16[128,96]{1,0:T(8,128)(2,1)S(1)}, bf16[128,96]{1,0:T(8,128)(2,1)}, u32[]{:S(2)}) copy-start(bf16[128,96]{1,0:T(8,128)(2,1)} %constant.25.clone.first_real) | copy-start | bytes 73732
  12.8 0.7 %copy-start.13 = (f32[3,7,256]{2,1,0:T(8,128)S(1)}, f32[3,7,256]{2,1,0:T(8,128)}, u32[]{:S(2)}) copy-start(f32[3,7,256]{2,1,0:T(8,128)} %short_filters.1) | copy-start | bytes 64516

commit v2 on v1

--- a/solution.py
+++ b/solution.py
@@ -213,6 +213,7 @@
 BF16 = jnp.bfloat16
 F32 = jnp.float32
 LANES = 128
+OPERANDS = 15
 
 
 def split16(value):
@@ -314,39 +315,42 @@
     return pltpu.roll(jnp.concatenate([value, zeros], axis=1), length + LANES - by, 1)[:, :length]
 
 
-def kernel(
-    filter_scale,
-    streams,
-    out_grad,
-    long_filter,
-    short_filters,
-    skip_gain,
-    order,
-    order_t,
-    filter_order,
-    filter_order_t,
-    first_cat,
-    first_real,
-    last_cat,
-    inner,
-    inner_back,
-    twiddles,
-    stream_grad,
-    filter_grad,
-    sent,
-    held,
-    answers,
-    results,
-    signal_rows,
-    filter_rows,
-    own_part,
-    other_part,
-    send_sem,
-    recv_sem,
-    back_send_sem,
-    back_recv_sem,
-    part_sem,
-):
+def kernel(filter_scale, *refs):
+    operands, refs = refs[:OPERANDS], refs[OPERANDS:]
+    stream_grad, filter_grad = refs[:2]
+    (
+        streams,
+        out_grad,
+        long_filter,
+        short_filters,
+        skip_gain,
+        order,
+        order_t,
+        filter_order,
+        filter_order_t,
+        first_cat,
+        first_real,
+        last_cat,
+        inner,
+        inner_back,
+        twiddles,
+    ) = locals_ = refs[2 : 2 + OPERANDS]
+    (
+        sent,
+        held,
+        answers,
+        results,
+        signal_rows,
+        filter_rows,
+        own_part,
+        other_part,
+        send_sem,
+        recv_sem,
+        back_send_sem,
+        back_recv_sem,
+        part_sem,
+        load_sem,
+    ) = refs[2 + OPERANDS :]
     devices = sent.shape[0]
     rows = sent.shape[1]
     length = streams.shape[2]
@@ -368,6 +372,17 @@
             barrier, inc=1, device_id={"seq": lax.rem(me + step, devices)}, device_id_type=MESH
         )
     pl.semaphore_signal(barrier, inc=1, device_id={"chan": other}, device_id_type=MESH)
+
+    loads = [
+        pltpu.make_async_copy(operands[index], locals_[index], load_sem.at[index])
+        for index in range(OPERANDS)
+    ]
+    first = (5, 0, 1, 7, 2)
+    later = [index for index in range(OPERANDS) if index not in first]
+    for index in first + tuple(later):
+        loads[index].start()
+    for index in first:
+        loads[index].wait()
 
     for index in range(4):
         block = out_grad[...] if index == 3 else streams[index]
@@ -413,6 +428,8 @@
             ).wait_recv()
 
     copies = exchange(sent, held, send_sem, recv_sem)
+    for index in later:
+        loads[index].wait()
     picked = order[pl.ds(pl.multiple_of(me * rows, rows), rows), :].astype(F32)
 
     def own_columns(values):
@@ -627,9 +644,10 @@
             jax.ShapeDtypeStruct(streams.shape, BF16),
             jax.ShapeDtypeStruct(long_filter.shape, F32),
         ),
-        in_specs=[vmem] * len(arguments),
+        in_specs=[pl.BlockSpec(memory_space=pltpu.HBM)] * len(arguments),
         out_specs=(vmem, vmem),
-        scratch_shapes=[
+        scratch_shapes=[pltpu.VMEM(value.shape, value.dtype) for value in arguments]
+        + [
             pltpu.VMEM((devices, rows, width), BF16),
             pltpu.VMEM((devices, rows, width), BF16),
             pltpu.VMEM((devices, rows, width_back), BF16),
@@ -643,9 +661,10 @@
             pltpu.SemaphoreType.DMA((devices,)),
             pltpu.SemaphoreType.DMA((devices,)),
             pltpu.SemaphoreType.DMA((2,)),
+            pltpu.SemaphoreType.DMA((OPERANDS,)),
         ],
         compiler_params=pltpu.CompilerParams(
-            collective_id=0, has_side_effects=True, vmem_limit_bytes=48 * 2**20
+            collective_id=0, has_side_effects=True, vmem_limit_bytes=62 * 2**20
         ),
     )(*arguments)
 

time: 51.2 us -> 39.8 us (0.78)
  local copies, waits for them, and re-layouts: 14.3 us -> 2.43 us
  Pallas kernels: 35.7 us -> 36.5 us
    unnamed x32 -> x4, local copies, waits for them, and re-layouts: 14.3 us -> 2.43 us
    pallas_call x1, Pallas kernels: 35.7 us -> 36.5 us  [fast_local(): pl.pallas_call(functools.partial(kernel, 1.0 / math.sqrt(members_total *...]
where the time goes in v2:
time: 39.8 us; the launch traced here: 39.6 us
  Pallas kernels  36.5 us (92%)
  local copies, waits for them, and re-layouts  2.43 us (6%)
  between operations  0.65 us (2%)
    pallas_call x1, Pallas kernels, fast_local(): pl.pallas_call(functools.partial(kernel, 1.0 / math.sqrt(members_total *...  36.5 us
    unnamed x4, local copies, waits for them, and re-layouts  2.43 us

profile of v2, /device:TPU:28, one launch (start us, length us, event | category | flops | bytes accessed | tf_op | source)
XLA Modules:
  0.0 39.6 jit_solution(9899159653832867668)
XLA Ops:
  0.6 36.5 %shard_map.158 = (bf16[3,256,256]{2,1,0:T(8,128)(2,1)}, f32[64,256]{1,0:T(8,128)}) custom-call(bf16[3,256,256]{2,1,0:T(8,128)(2,1)} %refs_0_.1, bf16[256,256]{1,0:T(8,128)(2,1)} %refs_1_.1, f32[64,256]{1,0:T(8,128)} %refs_2_.1, f32[3,7,256]{2,1,0:T(8,128)} %refs_3_.1, f32[1,256]{1,0:T(1,128)} %bitcast.1, bf16[256,256]{1,0:T(8,128)(2,1)} %constant.20.clone.refs_5_, ...), custom_call_target="tpu_custom_call" | custom-call | tf_op jit(solution)/shard_map/pallas_call | solution.py:641
  37.2 0.0 copy-start
  37.2 1.8 %copy.19 = bf16[3,256,256]{2,1,0:T(8,128)(2,1)} copy(bf16[3,256,256]{2,1,0:T(8,128)(2,1)} %get-tuple-element.4) | data formatting | bytes 786432
  39.0 0.0 copy-done
  39.0 0.6 %copy.20 = f32[64,256]{1,0:T(8,128)} copy(f32[64,256]{1,0:T(8,128)S(1)} %copy-done) | data formatting | bytes 131072
Async XLA Ops:
  37.2 1.8 %copy-start = (f32[64,256]{1,0:T(8,128)S(1)}, f32[64,256]{1,0:T(8,128)}, u32[]{:S(2)}) copy-start(f32[64,256]{1,0:T(8,128)} %get-tuple-element.5) | copy-start | bytes 196612

commit v3 on v2

--- a/solution.py
+++ b/solution.py
@@ -237,7 +237,16 @@
     members = channels // filters
     own_filters = filters // devices
     rows = np.arange(channels)
-    order = one_hot_rows(filters * (rows % members) + rows // members)
+    block = channels // devices
+    owner, side, within = rows // block, rows // (block // 2) % 2, rows % (block // 2)
+    gather = np.zeros((2, channels, 2 * channels), np.float32)
+    scatter = np.zeros((2, channels, 2 * channels), np.float32)
+    for chunk in range(2):
+        own = chunk * own_filters // 2 + within // members
+        channel = filters * (within % members) + own_filters * owner + own
+        gather[chunk, rows, side * channels + channel] = 1.0
+        scatter[side, channel, chunk * channels + rows] = 1.0
+    gather, scatter = gather.astype(ml_dtypes.bfloat16), scatter.astype(ml_dtypes.bfloat16)
     rows = np.arange(4 * filters)
     owner, kind, own = rows // (4 * own_filters), rows // own_filters % 4, rows % own_filters
     filter_order = one_hot_rows(kind * filters + owner * own_filters + own)
@@ -261,8 +270,8 @@
     angle = -2.0 * math.pi * np.outer(np.arange(outer), np.arange(LANES)) / fft_size
     twiddles = np.stack([np.cos(angle), np.sin(angle)]).astype(np.float32)
     return (
-        order,
-        np.ascontiguousarray(order.T),
+        gather,
+        scatter,
         filter_order,
         np.ascontiguousarray(filter_order.T),
         first_cat,
@@ -324,8 +333,8 @@
         long_filter,
         short_filters,
         skip_gain,
-        order,
-        order_t,
+        gather,
+        scatter,
         filter_order,
         filter_order_t,
         first_cat,
@@ -336,10 +345,14 @@
         twiddles,
     ) = locals_ = refs[2 : 2 + OPERANDS]
     (
-        sent,
-        held,
-        answers,
-        results,
+        sent_zero,
+        sent_one,
+        held_zero,
+        held_one,
+        answers_zero,
+        answers_one,
+        results_zero,
+        results_one,
         signal_rows,
         filter_rows,
         own_part,
@@ -351,18 +364,22 @@
         part_sem,
         load_sem,
     ) = refs[2 + OPERANDS :]
-    devices = sent.shape[0]
-    rows = sent.shape[1]
-    length = streams.shape[2]
+    devices = sent_one.shape[0]
+    rows = sent_one.shape[1]
+    half = rows // 2
+    channels, length = streams.shape[1:]
     filters = long_filter.shape[0]
     taps = short_filters.shape[1]
     own_filters = filters // devices
+    chunk_filters = own_filters // 2
     members = rows // own_filters
-    pairs = rows // 2
+    pairs = half // 2
     per_filter = members // 2
     used = devices * length // LANES
     outer = 2 * used
     pieces = length // LANES
+    sent, held = (sent_zero, sent_one), (held_zero, held_one)
+    answers, results = (answers_zero, answers_one), (results_zero, results_one)
     me = lax.axis_index("seq")
     other = 1 - lax.axis_index("chan")
 
@@ -384,29 +401,27 @@
     for index in first:
         loads[index].wait()
 
-    for index in range(4):
-        block = out_grad[...] if index == 3 else streams[index]
-        moved = dot32(order[...], block).astype(BF16)
-        sent[:, :, index * length : (index + 1) * length] = moved.reshape(devices, rows, length)
-    high, low = split16(long_filter[...])
-    stacked = []
-    for piece in range(pieces):
-        columns = slice(piece * LANES, (piece + 1) * LANES)
-        stacked += [high[:, columns], low[:, columns]]
-    moved = dot32(filter_order[...], jnp.concatenate(stacked, axis=0)).astype(BF16)
-    sent[:, :, 4 * length :] = moved.reshape(devices, rows, LANES)
-
-    pl.semaphore_wait(barrier, devices)
-
-    def exchange(source, target, send, recv):
+    blocks = (
+        jnp.concatenate([streams[0], streams[2]], axis=0),
+        jnp.concatenate([streams[1], out_grad[...]], axis=0),
+    )
+
+    def fill(chunk):
+        for index in range(2):
+            moved = dot32(gather[chunk], blocks[index]).astype(BF16)
+            sent[chunk][:, :, index * length : (index + 1) * length] = moved.reshape(
+                devices, rows, length
+            )
+
+    def exchange(source, target, send, recv, chunk):
         copies = []
         for step in range(1, devices):
             peer = lax.rem(me + step, devices)
             copy = pltpu.make_async_remote_copy(
                 src_ref=source.at[peer],
                 dst_ref=target.at[me],
-                send_sem=send.at[peer],
-                recv_sem=recv.at[me],
+                send_sem=send.at[chunk, peer],
+                recv_sem=recv.at[chunk, me],
                 device_id={"seq": peer},
                 device_id_type=MESH,
             )
@@ -415,22 +430,37 @@
         target[me] = source[me]
         return copies
 
-    def finish(copies, source, target, send, recv):
+    def finish(source, target, send, recv, chunk):
         for step in range(1, devices):
             peer = lax.rem(me + step, devices)
             pltpu.make_async_remote_copy(
                 src_ref=source.at[peer],
                 dst_ref=target.at[peer],
-                send_sem=send.at[peer],
-                recv_sem=recv.at[peer],
+                send_sem=send.at[chunk, peer],
+                recv_sem=recv.at[chunk, peer],
                 device_id={"seq": peer},
                 device_id_type=MESH,
             ).wait_recv()
 
-    copies = exchange(sent, held, send_sem, recv_sem)
+    fill(0)
+    high, low = split16(long_filter[...])
+    stacked = []
+    for piece in range(pieces):
+        columns = slice(piece * LANES, (piece + 1) * LANES)
+        stacked += [high[:, columns], low[:, columns]]
+    moved = dot32(filter_order[...], jnp.concatenate(stacked, axis=0)).astype(BF16)
+    sent_zero[:, :, 2 * length :] = moved.reshape(devices, rows, LANES)
+    pl.semaphore_wait(barrier, devices)
+    copies = exchange(sent_zero, held_zero, send_sem, recv_sem, 0)
+    fill(1)
+    copies += exchange(sent_one, held_one, send_sem, recv_sem, 1)
+
     for index in later:
         loads[index].wait()
-    picked = order[pl.ds(pl.multiple_of(me * rows, rows), rows), :].astype(F32)
+    own_rows = pl.ds(pl.multiple_of(me * rows, rows), rows)
+    picked = jnp.concatenate(
+        [gather[chunk, own_rows, :channels].astype(F32)[:half] for chunk in range(2)], axis=0
+    )
 
     def own_columns(values):
         return lax.dot_general(
@@ -441,85 +471,27 @@
             preferred_element_type=F32,
         )
 
-    weights = [own_columns(short_filters[index]) for index in range(3)]
-    gain = jnp.sum(picked * skip_gain[...], axis=1, keepdims=True)
-    finish(copies, sent, held, send_sem, recv_sem)
-
-    def whole(index):
-        columns = slice(index * length, (index + 1) * length)
-        return jnp.concatenate(
-            [held[source, :, columns].astype(F32) for source in range(devices)], axis=1
-        )
-
-    filtered = []
-    for index in range(3):
-        value = whole(index)
-        total = weights[index][:, 0:1] * value
-        for offset in range(1, taps):
-            total = total + weights[index][:, offset : offset + 1] * delayed(value, offset)
-        filtered.append(total)
-    out_float = whole(3)
-    gated_prod = filtered[1] * filtered[2]
-    gate_grad = out_float * filtered[0]
-    for block in range(used):
-        columns = slice(block * LANES, (block + 1) * LANES)
-        signal_rows[0, block * rows : (block + 1) * rows, :] = gated_prod[:, columns]
-        signal_rows[1, block * rows : (block + 1) * rows, :] = gate_grad[:, columns]
-    for source in range(devices):
-        filter_rows[source * rows : (source + 1) * rows, :] = held[source, :, 4 * length :].astype(
-            F32
-        )
-
-    def channel_rows(which, channel):
-        return signal_rows[which, pl.ds(channel, used, stride=rows), :]
-
-    stride = 2 * own_filters
-
-    def filter_part(part):
-        return jnp.concatenate(
-            [
-                filter_rows[pl.ds(part * own_filters + own, used, stride=stride), :]
-                for own in range(own_filters)
-            ],
-            axis=1,
-        ).astype(BF16)
-
-    def packed(which, part):
-        return [channel_rows(which, 2 * pair + part) for pair in range(pairs)]
-
-    signals = jnp.concatenate(
-        [
-            jnp.concatenate(packed(0, part) + packed(1, part), axis=1)
-            for part in range(2)
-        ],
-        axis=0,
-    )
-    part_high, part_low = filter_part(0), filter_part(1)
-    outer_out = jnp.concatenate(
-        [
-            outer_product(first_cat[...], signals),
-            dot32(first_real[...], jnp.concatenate([part_high, part_high, part_low], axis=0)),
-        ],
-        axis=1,
-    )
+    all_weights = [own_columns(short_filters[index]) for index in range(3)]
+    all_gain = jnp.sum(picked * skip_gain[...], axis=1, keepdims=True)
     twiddle_re, twiddle_im = twiddles[0], twiddles[1]
-    count = 2 * pairs + own_filters
-    turned = []
-    for index in range(count):
-        columns = slice(index * LANES, (index + 1) * LANES)
-        real_part, imag_part = outer_out[:outer, columns], outer_out[outer:, columns]
-        turned.append(
-            jnp.concatenate(
-                [
-                    real_part * twiddle_re - imag_part * twiddle_im,
-                    real_part * twiddle_im + imag_part * twiddle_re,
-                ],
-                axis=1,
+
+    def forward(outer_out):
+        turned = []
+        for index in range(outer_out.shape[1] // LANES):
+            columns = slice(index * LANES, (index + 1) * LANES)
+            real_part, imag_part = outer_out[:outer, columns], outer_out[outer:, columns]
+            turned.append(
+                jnp.concatenate(
+                    [
+                        real_part * twiddle_re - imag_part * twiddle_im,
+                        real_part * twiddle_im + imag_part * twiddle_re,
+                    ],
+                    axis=1,
+                )
             )
-        )
-    spectra = inner_product(jnp.concatenate(turned, axis=0), inner)
-
-    def spectrum(index):
+        return inner_product(jnp.concatenate(turned, axis=0), inner)
+
+    def spectrum(spectra, index):
         return spectra[index * outer : (index + 1) * outer]
 
     def inverse(values, table):
@@ -538,76 +510,172 @@
             )
         return outer_product(table, jnp.concatenate(columns, axis=1))
 
-    sums = []
-    for own in range(own_filters):
-        total = None
-        for index in range(own * per_filter, (own + 1) * per_filter):
-            term = product(spectrum(pairs + index), spectrum(index), True)
-            total = term if total is None else total + term
-        sums.append(total)
-    own_part[...] = inverse(sums, last_cat[:used, :])
-    part_copy = pltpu.make_async_remote_copy(
-        src_ref=own_part,
-        dst_ref=other_part,
-        send_sem=part_sem.at[0],
-        recv_sem=part_sem.at[1],
-        device_id={"chan": other},
-        device_id_type=MESH,
-    )
-    part_copy.start()
-
-    products = []
-    for index in range(2 * pairs):
-        filter_spec = spectrum(2 * pairs + index % pairs // per_filter)
-        products.append(product(spectrum(index), filter_spec, index >= pairs))
-    times = inverse(products, last_cat[...])
-    for index in range(2 * pairs):
-        which, pair = index // pairs, index % pairs
-        columns = slice(index * LANES, (index + 1) * LANES)
-        for part in range(2):
-            signal_rows[which, pl.ds(2 * pair + part, used, stride=rows), :] = times[
-                part * used : (part + 1) * used, columns
+    def filter_spectra():
+        for source in range(devices):
+            filter_rows[source * rows : (source + 1) * rows, :] = held_zero[
+                source, :, 2 * length :
+            ].astype(F32)
+        high, low = [
+            jnp.concatenate(
+                [
+                    filter_rows[pl.ds(part * own_filters + own, used, stride=stride), :]
+                    for own in range(own_filters)
+                ],
+                axis=1,
+            ).astype(BF16)
+            for part in range(2)
+        ]
+        return forward(dot32(first_real[...], jnp.concatenate([high, high, low], axis=0)))
+
+    stride = 2 * own_filters
+
+    def work(chunk, filter_specs):
+        weights = [value[chunk * half : (chunk + 1) * half] for value in all_weights]
+        gain = all_gain[chunk * half : (chunk + 1) * half]
+        received = held[chunk]
+
+        def whole(side, index):
+            columns = slice(index * length, (index + 1) * length)
+            return jnp.concatenate(
+                [
+                    received[source, :, columns].astype(F32)[side * half : (side + 1) * half]
+                    for source in range(devices)
+                ],
+                axis=1,
+            )
+
+        filtered = []
+        for index, place in enumerate(((0, 0), (0, 1), (1, 0))):
+            value = whole(*place)
+            total = weights[index][:, 0:1] * value
+            for offset in range(1, taps):
+                total = total + weights[index][:, offset : offset + 1] * delayed(value, offset)
+            filtered.append(total)
+        out_float = whole(1, 1)
+        gated_prod = filtered[1] * filtered[2]
+        gate_grad = out_float * filtered[0]
+        for block in range(used):
+            columns = slice(block * LANES, (block + 1) * LANES)
+            span = slice(block * half, (block + 1) * half)
+            signal_rows[chunk, 0, span, :] = gated_prod[:, columns]
+            signal_rows[chunk, 1, span, :] = gate_grad[:, columns]
+
+        def packed(which, part):
+            return [
+                signal_rows[chunk, which, pl.ds(2 * pair + part, used, stride=half), :]
+                for pair in range(pairs)
             ]
 
-    def joined(which):
-        return jnp.concatenate(
-            [signal_rows[which, block * rows : (block + 1) * rows, :] for block in range(used)],
-            axis=1,
-        )
-
-    conv_out = joined(0) + gain * gated_prod
-    gated_grad = joined(1) + gain * gate_grad
-    grads = (out_float * conv_out, gated_grad * filtered[2], gated_grad * filtered[1])
-    for index in range(3):
-        value = grads[index]
-        total = weights[index][:, 0:1] * value
-        for offset in range(1, taps):
-            total = total + weights[index][:, offset : offset + 1] * advanced(value, offset)
-        total = total.astype(BF16)
+        signals = jnp.concatenate(
+            [jnp.concatenate(packed(0, part) + packed(1, part), axis=1) for part in range(2)],
+            axis=0,
+        )
+        spectra = forward(outer_product(first_cat[...], signals))
+        sums = []
+        for own in range(chunk_filters):
+            total = None
+            for index in range(own * per_filter, (own + 1) * per_filter):
+                term = product(spectrum(spectra, pairs + index), spectrum(spectra, index), True)
+                total = term if total is None else total + term
+            sums.append(total)
+        own_part[chunk] = inverse(sums, last_cat[:used, :])
+        part_copy = pltpu.make_async_remote_copy(
+            src_ref=own_part.at[chunk],
+            dst_ref=other_part.at[chunk],
+            send_sem=part_sem.at[0, chunk],
+            recv_sem=part_sem.at[1, chunk],
+            device_id={"chan": other},
+            device_id_type=MESH,
+        )
+        part_copy.start()
+
+        products = []
+        for index in range(2 * pairs):
+            own = chunk * chunk_filters + index % pairs // per_filter
+            products.append(
+                product(spectrum(spectra, index), spectrum(filter_specs, own), index >= pairs)
+            )
+        times = inverse(products, last_cat[...])
+        for index in range(2 * pairs):
+            which, pair = index // pairs, index % pairs
+            columns = slice(index * LANES, (index + 1) * LANES)
+            for part in range(2):
+                signal_rows[chunk, which, pl.ds(2 * pair + part, used, stride=half), :] = times[
+                    part * used : (part + 1) * used, columns
+                ]
+
+        def joined(which):
+            return jnp.concatenate(
+                [
+                    signal_rows[chunk, which, block * half : (block + 1) * half, :]
+                    for block in range(used)
+                ],
+                axis=1,
+            )
+
+        conv_out = joined(0) + gain * gated_prod
+        gated_grad = joined(1) + gain * gate_grad
+        grads = (out_float * conv_out, gated_grad * filtered[2], gated_grad * filtered[1])
+        totals = []
+        for index in range(3):
+            value = grads[index]
+            total = weights[index][:, 0:1] * value
+            for offset in range(1, taps):
+                total = total + weights[index][:, offset : offset + 1] * advanced(value, offset)
+            totals.append(total)
+        both = jnp.concatenate(totals[:2], axis=0).astype(BF16)
         for target in range(devices):
-            answers[target, :, index * length : (index + 1) * length] = total[
-                :, target * length : (target + 1) * length
-            ]
-
-    part_copy.wait()
-    high, low = split16((own_part[...] + other_part[...]) * filter_scale)
-    for own in range(own_filters):
-        columns = slice(own * LANES, (own + 1) * LANES)
-        filter_rows[pl.ds(own, used, stride=stride), :] = high[:, columns].astype(F32)
-        filter_rows[pl.ds(own_filters + own, used, stride=stride), :] = low[:, columns].astype(F32)
+            start = target * length
+            answers[chunk][target, :, :length] = both[:, start : start + length]
+            answers[chunk][target, :, length : length + LANES] = jnp.concatenate(
+                [
+                    totals[2][:, start : start + LANES],
+                    totals[2][:, start + LANES : start + 2 * LANES],
+                ],
+                axis=0,
+            ).astype(BF16)
+        return part_copy
+
+    finish(sent_zero, held_zero, send_sem, recv_sem, 0)
+    filter_specs = filter_spectra()
+    part_copies = [work(0, filter_specs)]
+    back_copies = exchange(answers_zero, results_zero, back_send_sem, back_recv_sem, 0)
+    finish(sent_one, held_one, send_sem, recv_sem, 1)
+    part_copies.append(work(1, filter_specs))
+
+    for copy in part_copies:
+        copy.wait()
+    for chunk in range(2):
+        high, low = split16((own_part[chunk] + other_part[chunk]) * filter_scale)
+        for index in range(chunk_filters):
+            columns = slice(index * LANES, (index + 1) * LANES)
+            own = chunk * chunk_filters + index
+            filter_rows[pl.ds(own, used, stride=stride), :] = high[:, columns].astype(F32)
+            filter_rows[pl.ds(own_filters + own, used, stride=stride), :] = low[
+                :, columns
+            ].astype(F32)
     for target in range(devices):
-        answers[target, :, 3 * length :] = filter_rows[
+        answers_one[target, :, length + LANES :] = filter_rows[
             target * rows : (target + 1) * rows, :
         ].astype(BF16)
-
-    back_copies = exchange(answers, results, back_send_sem, back_recv_sem)
+    back_copies += exchange(answers_one, results_one, back_send_sem, back_recv_sem, 1)
     for copy in copies:
         copy.wait_send()
-    finish(back_copies, answers, results, back_send_sem, back_recv_sem)
-    for index in range(3):
-        block = results[:, :, index * length : (index + 1) * length].reshape(devices * rows, length)
-        stream_grad[index] = dot32(order_t[...], block).astype(BF16)
-    block = results[:, :, 3 * length :].reshape(devices * rows, LANES)
+    for chunk in range(2):
+        finish(answers[chunk], results[chunk], back_send_sem, back_recv_sem, chunk)
+
+    def returned(columns):
+        return jnp.concatenate(
+            [results[chunk][:, :, columns].reshape(devices * rows, -1) for chunk in range(2)],
+            axis=0,
+        )
+
+    for side in range(2):
+        stream_grad[side] = dot32(scatter[side], returned(slice(0, length))).astype(BF16)
+        stream_grad[2, :, side * LANES : (side + 1) * LANES] = dot32(
+            scatter[side], returned(slice(length, length + LANES))
+        ).astype(BF16)
+    block = results_one[:, :, length + LANES :].reshape(devices * rows, LANES)
     moved = dot32(filter_order_t[...], block)
     for piece in range(pieces):
         start = 2 * piece * filters
@@ -636,8 +704,6 @@
         skip_gain.reshape(1, channels),
     ] + constants
     vmem = pl.BlockSpec(memory_space=pltpu.VMEM)
-    width = 4 * length + LANES
-    width_back = 3 * length + LANES
     return pl.pallas_call(
         functools.partial(kernel, 1.0 / math.sqrt(members_total * tokens)),
         out_shape=(
@@ -648,19 +714,23 @@
         out_specs=(vmem, vmem),
         scratch_shapes=[pltpu.VMEM(value.shape, value.dtype) for value in arguments]
         + [
-            pltpu.VMEM((devices, rows, width), BF16),
-            pltpu.VMEM((devices, rows, width), BF16),
-            pltpu.VMEM((devices, rows, width_back), BF16),
-            pltpu.VMEM((devices, rows, width_back), BF16),
-            pltpu.VMEM((2, used * rows, LANES), F32),
+            pltpu.VMEM((devices, rows, 2 * length + LANES), BF16),
+            pltpu.VMEM((devices, rows, 2 * length), BF16),
+            pltpu.VMEM((devices, rows, 2 * length + LANES), BF16),
+            pltpu.VMEM((devices, rows, 2 * length), BF16),
+            pltpu.VMEM((devices, rows, length + LANES), BF16),
+            pltpu.VMEM((devices, rows, length + 2 * LANES), BF16),
+            pltpu.VMEM((devices, rows, length + LANES), BF16),
+            pltpu.VMEM((devices, rows, length + 2 * LANES), BF16),
+            pltpu.VMEM((2, 2, used * rows // 2, LANES), F32),
             pltpu.VMEM((devices * rows, LANES), F32),
-            pltpu.VMEM((used, own_filters * LANES), F32),
-            pltpu.VMEM((used, own_filters * LANES), F32),
-            pltpu.SemaphoreType.DMA((devices,)),
-            pltpu.SemaphoreType.DMA((devices,)),
-            pltpu.SemaphoreType.DMA((devices,)),
-            pltpu.SemaphoreType.DMA((devices,)),
-            pltpu.SemaphoreType.DMA((2,)),
+            pltpu.VMEM((2, used, own_filters // 2 * LANES), F32),
+            pltpu.VMEM((2, used, own_filters // 2 * LANES), F32),
+            pltpu.SemaphoreType.DMA((2, devices)),
+            pltpu.SemaphoreType.DMA((2, devices)),
+            pltpu.SemaphoreType.DMA((2, devices)),
+            pltpu.SemaphoreType.DMA((2, devices)),
+            pltpu.SemaphoreType.DMA((2, 2)),
             pltpu.SemaphoreType.DMA((OPERANDS,)),
         ],
         compiler_params=pltpu.CompilerParams(
@@ -674,7 +744,7 @@
     channels, length = channels // groups, tokens // devices
     if groups != 2 or filters % devices or channels % (2 * filters) or channels % (16 * devices):
         return False
-    return length == 2 * LANES and channels // devices == 4 * (filters // devices)
+    return length == 2 * LANES and channels // devices == 4 * (filters // devices) == 16
 
 
 def solution(mesh):

time: 39.8 us -> 38.8 us (0.975)
  the two profiles are of different devices: /device:TPU:28 before, /device:TPU:0 now
where the time goes in v3:
time: 38.8 us; the launch traced here: 38.6 us
  Pallas kernels  35.6 us (92%)
  local copies, waits for them, and re-layouts  2.43 us (6%)
  between operations  0.65 us (2%)
    pallas_call x1, Pallas kernels, fast_local(): pl.pallas_call(functools.partial(kernel, 1.0 / math.sqrt(members_total *...  35.6 us
    unnamed x4, local copies, waits for them, and re-layouts  2.43 us

profile of v3, /device:TPU:0, one launch (start us, length us, event | category | flops | bytes accessed | tf_op | source)
XLA Modules:
  0.0 38.6 jit_solution(1235905183074635895)
XLA Ops:
  0.6 35.6 %shard_map.158 = (bf16[3,256,256]{2,1,0:T(8,128)(2,1)}, f32[64,256]{1,0:T(8,128)}) custom-call(bf16[3,256,256]{2,1,0:T(8,128)(2,1)} %refs_0_.1, bf16[256,256]{1,0:T(8,128)(2,1)} %refs_1_.1, f32[64,256]{1,0:T(8,128)} %refs_2_.1, f32[3,7,256]{2,1,0:T(8,128)} %refs_3_.1, f32[1,256]{1,0:T(1,128)} %bitcast.1, bf16[2,256,512]{2,1,0:T(8,128)(2,1)} %constant.20.clone.refs_5_, ...), custom_call_target="tpu_custom_call" | custom-call | tf_op jit(solution)/shard_map/pallas_call | solution.py:707
  36.2 0.0 copy-start
  36.2 1.8 %copy.19 = bf16[3,256,256]{2,1,0:T(8,128)(2,1)} copy(bf16[3,256,256]{2,1,0:T(8,128)(2,1)} %get-tuple-element.4) | data formatting | bytes 786432
  38.0 0.0 copy-done
  38.0 0.6 %copy.20 = f32[64,256]{1,0:T(8,128)} copy(f32[64,256]{1,0:T(8,128)S(1)} %copy-done) | data formatting | bytes 131072
Async XLA Ops:
  36.2 1.8 %copy-start = (f32[64,256]{1,0:T(8,128)S(1)}, f32[64,256]{1,0:T(8,128)}, u32[]{:S(2)}) copy-start(f32[64,256]{1,0:T(8,128)} %get-tuple-element.5) | copy-start | bytes 196612

commit v4 on v3

--- a/solution.py
+++ b/solution.py
@@ -363,6 +363,7 @@
         back_recv_sem,
         part_sem,
         load_sem,
+        gather_sem,
     ) = refs[2 + OPERANDS :]
     devices = sent_one.shape[0]
     rows = sent_one.shape[1]
@@ -394,10 +395,20 @@
         pltpu.make_async_copy(operands[index], locals_[index], load_sem.at[index])
         for index in range(OPERANDS)
     ]
-    first = (5, 0, 1, 7, 2)
-    later = [index for index in range(OPERANDS) if index not in first]
-    for index in first + tuple(later):
+    gather_place = 5
+    gather_loads = [
+        pltpu.make_async_copy(
+            operands[gather_place].at[chunk], gather.at[chunk], gather_sem.at[chunk]
+        )
+        for chunk in range(2)
+    ]
+    first = (0, 1, 7, 2)
+    later = [index for index in range(OPERANDS) if index not in first + (gather_place,)]
+    gather_loads[0].start()
+    for index in first:
         loads[index].start()
+    gather_loads[1].start()
+    gather_loads[0].wait()
     for index in first:
         loads[index].wait()
 
@@ -452,6 +463,9 @@
     sent_zero[:, :, 2 * length :] = moved.reshape(devices, rows, LANES)
     pl.semaphore_wait(barrier, devices)
     copies = exchange(sent_zero, held_zero, send_sem, recv_sem, 0)
+    for index in later:
+        loads[index].start()
+    gather_loads[1].wait()
     fill(1)
     copies += exchange(sent_one, held_one, send_sem, recv_sem, 1)
 
@@ -732,6 +746,7 @@
             pltpu.SemaphoreType.DMA((2, devices)),
             pltpu.SemaphoreType.DMA((2, 2)),
             pltpu.SemaphoreType.DMA((OPERANDS,)),
+            pltpu.SemaphoreType.DMA((2,)),
         ],
         compiler_params=pltpu.CompilerParams(
             collective_id=0, has_side_effects=True, vmem_limit_bytes=62 * 2**20

time: 38.8 us -> 38.8 us (level)
  no operation moved by 1% of the time
where the time goes in v4:
time: 38.8 us; the launch traced here: 38.6 us
  Pallas kernels  35.6 us (92%)
  local copies, waits for them, and re-layouts  2.43 us (6%)
  between operations  0.65 us (2%)
    pallas_call x1, Pallas kernels, fast_local(): pl.pallas_call(functools.partial(kernel, 1.0 / math.sqrt(members_total *...  35.6 us
    unnamed x4, local copies, waits for them, and re-layouts  2.43 us

profile of v4, /device:TPU:0, one launch (start us, length us, event | category | flops | bytes accessed | tf_op | source)
XLA Modules:
  0.0 38.6 jit_solution(5860660683824645247)
XLA Ops:
  0.6 35.6 %shard_map.158 = (bf16[3,256,256]{2,1,0:T(8,128)(2,1)}, f32[64,256]{1,0:T(8,128)}) custom-call(bf16[3,256,256]{2,1,0:T(8,128)(2,1)} %refs_0_.1, bf16[256,256]{1,0:T(8,128)(2,1)} %refs_1_.1, f32[64,256]{1,0:T(8,128)} %refs_2_.1, f32[3,7,256]{2,1,0:T(8,128)} %refs_3_.1, f32[1,256]{1,0:T(1,128)} %bitcast.1, bf16[2,256,512]{2,1,0:T(8,128)(2,1)} %constant.20.clone.refs_5_, ...), custom_call_target="tpu_custom_call" | custom-call | tf_op jit(solution)/shard_map/pallas_call | solution.py:721
  36.2 0.0 copy-start
  36.2 1.8 %copy.19 = bf16[3,256,256]{2,1,0:T(8,128)(2,1)} copy(bf16[3,256,256]{2,1,0:T(8,128)(2,1)} %get-tuple-element.4) | data formatting | bytes 786432
  38.0 0.0 copy-done
  38.0 0.6 %copy.20 = f32[64,256]{1,0:T(8,128)} copy(f32[64,256]{1,0:T(8,128)S(1)} %copy-done) | data formatting | bytes 131072
Async XLA Ops:
  36.2 1.8 %copy-start = (f32[64,256]{1,0:T(8,128)S(1)}, f32[64,256]{1,0:T(8,128)}, u32[]{:S(2)}) copy-start(f32[64,256]{1,0:T(8,128)} %get-tuple-element.5) | copy-start | bytes 196612

commit v5 on v4

--- a/solution.py
+++ b/solution.py
@@ -427,7 +427,7 @@
     def exchange(source, target, send, recv, chunk):
         copies = []
         for step in range(1, devices):
-            peer = lax.rem(me + step, devices)
+            peer = lax.rem(me + step + (1 - other) * (devices - 2 * step), devices)
             copy = pltpu.make_async_remote_copy(
                 src_ref=source.at[peer],
                 dst_ref=target.at[me],
@@ -443,7 +443,7 @@
 
     def finish(source, target, send, recv, chunk):
         for step in range(1, devices):
-            peer = lax.rem(me + step, devices)
+            peer = lax.rem(me + step + (1 - other) * (devices - 2 * step), devices)
             pltpu.make_async_remote_copy(
                 src_ref=source.at[peer],
                 dst_ref=target.at[peer],

time: 38.8 us -> 40.2 us (1.036)
  the two profiles are of different devices: /device:TPU:0 before, /device:TPU:1 now
where the time goes in v5:
time: 40.2 us; the launch traced here: 40.1 us
  Pallas kernels  37 us (92%)
  local copies, waits for them, and re-layouts  2.43 us (6%)
  between operations  0.65 us (2%)
    pallas_call x1, Pallas kernels, fast_local(): pl.pallas_call(functools.partial(kernel, 1.0 / math.sqrt(members_total *...  37 us
    unnamed x4, local copies, waits for them, and re-layouts  2.43 us

profile of v5, /device:TPU:1, one launch (start us, length us, event | category | flops | bytes accessed | tf_op | source)
XLA Modules:
  0.0 40.1 jit_solution(6909741318932521660)
XLA Ops:
  0.6 37.0 %shard_map.158 = (bf16[3,256,256]{2,1,0:T(8,128)(2,1)}, f32[64,256]{1,0:T(8,128)}) custom-call(bf16[3,256,256]{2,1,0:T(8,128)(2,1)} %refs_0_.1, bf16[256,256]{1,0:T(8,128)(2,1)} %refs_1_.1, f32[64,256]{1,0:T(8,128)} %refs_2_.1, f32[3,7,256]{2,1,0:T(8,128)} %refs_3_.1, f32[1,256]{1,0:T(1,128)} %bitcast.1, bf16[2,256,512]{2,1,0:T(8,128)(2,1)} %constant.20.clone.refs_5_, ...), custom_call_target="tpu_custom_call" | custom-call | tf_op jit(solution)/shard_map/pallas_call | solution.py:721
  37.6 0.0 copy-start
  37.6 1.8 %copy.19 = bf16[3,256,256]{2,1,0:T(8,128)(2,1)} copy(bf16[3,256,256]{2,1,0:T(8,128)(2,1)} %get-tuple-element.4) | data formatting | bytes 786432
  39.4 0.0 copy-done
  39.4 0.6 %copy.20 = f32[64,256]{1,0:T(8,128)} copy(f32[64,256]{1,0:T(8,128)S(1)} %copy-done) | data formatting | bytes 131072
Async XLA Ops:
  37.6 1.8 %copy-start = (f32[64,256]{1,0:T(8,128)S(1)}, f32[64,256]{1,0:T(8,128)}, u32[]{:S(2)}) copy-start(f32[64,256]{1,0:T(8,128)} %get-tuple-element.5) | copy-start | bytes 196612
